TPU v7x, 128 devices: a whole 4x4x4 slice. The times are simulated.
128 devices in a mesh: expert: 32 (over x, z, core), tensor: 4 (over y).
Axes of the slice: x: 4, y: 4, z: 4, core: 2. Of those that a mesh axis runs over, the one named last changes fastest.
Arguments:
- tokens: bfloat16 [16384, 2048], P('expert'), may hold values from -40 to 40
- norm_gain: float32 [2048], replicated, may hold values from 0.5 to 1.5
- expert_ids: int32 [16384, 8], P('expert'), may hold values from 0 to 127, all different within a row; in each aligned block of 512 rows (0 to 511, 512 to 1023, ...) at most 34 rows name the same one
- route_weights: float32 [16384, 8], P('expert'), may hold values from 0.5 to 1
- w_gate: bfloat16 [128, 2048, 768], P('expert', None, 'tensor'), may hold values from -0.125 to 0.125
- w_up: bfloat16 [128, 2048, 768], P('expert', None, 'tensor'), may hold values from -0.125 to 0.125
- w_down: bfloat16 [128, 768, 2048], P('expert', 'tensor'), may hold values from -0.21875 to 0.21875
- codec_embeds: bfloat16 [32768, 1024], P(('expert', 'tensor')), may hold values from -30 to 30
- frame_lengths: int32 [64], P('expert'), may hold values from 128 to 896, as said below
- source_rows: int32 [32768], P(('expert', 'tensor')), may hold values from 0 to 16383, as said below
- w_handover: bfloat16 [2048, 1024], replicated, may hold values from -0.125 to 0.125
- talker_gain: float32 [1024], replicated, may hold values from 0.5 to 1.5
- w_query: bfloat16 [1024, 1024], replicated, may hold values from -1 to 1
- w_kv: bfloat16 [1024, 1024], replicated, may hold values from -1 to 1
- qk_gains: float32 [2, 128], replicated, may hold values from 1 to 5
- w_out: bfloat16 [1024, 1024], replicated, may hold values from -0.1875 to 0.1875
Outputs:
- thinker_out: bfloat16 [16384, 2048], P(('expert', 'tensor'))
- talker_out: bfloat16 [32768, 1024], P(('expert', 'tensor'))
Inputs may be any that keep to these rules, and one draw needn't show every extreme that they name: `expert_ids`: in each aligned block of 512 tokens no expert is named by more than 34 routes, and in every draw some expert is named by exactly 34 routes of some block. `frame_lengths`: entries 2 g and 2 g + 1 are the frame counts of the two dialogues of group g and sum to 1024. `source_rows`: A frame of group g reads one of the thinker rows g * 512 to (g + 1) * 512 - 1; along the frames of one dialogue the rows never fall.
All inputs are finite; a program needn't handle non-finite values.
Results may differ from a plain program's by a relative error of at most 0.04.
Values may be sent and summed in bfloat16 or wider, within the bound.
A program may use at most 192 MiB of HBM per device.

v0:
```python
import jax
import jax.numpy as jnp
from jax import lax
from jax.sharding import PartitionSpec as P

HEADS = 8
KV_HEADS = 4
HEAD = 128


epsilon = 1e-06


def rms_scale(values, gain):
    mean_square = jnp.mean(values * values, axis=-1, keepdims=True)
    return values * lax.rsqrt(mean_square + epsilon) * gain


def route_slots(expert_ids, expert_count, capacity):
    token_count, top_count = expert_ids.shape
    flat_ids = expert_ids.reshape(token_count * top_count)
    one_hot = (flat_ids[:, None] == jnp.arange(expert_count, dtype=jnp.int32)[None, :]).astype(
        jnp.int32
    )
    before = jnp.cumsum(one_hot, axis=0) - one_hot
    slot_rank = jnp.sum(before * one_hot, axis=1)
    return flat_ids * capacity + slot_rank


def per_device(
    tokens,
    norm_gain,
    expert_ids,
    route_weights,
    w_gate,
    w_up,
    w_down,
    codec_embeds,
    frame_lengths,
    source_rows,
    w_handover,
    talker_gain,
    w_query,
    w_kv,
    qk_gains,
    w_out,
):
    groups = lax.axis_size("expert")
    tensor_count = lax.axis_size("tensor")
    group_index = lax.axis_index("expert")
    tensor_index = lax.axis_index("tensor")
    local_experts = w_gate.shape[0]
    expert_count = local_experts * groups
    token_count, top_count = expert_ids.shape
    capacity = 17 * token_count * top_count // (16 * expert_count)
    model_width = tokens.shape[1]
    normed = rms_scale(tokens.astype(jnp.float32), norm_gain).astype(jnp.bfloat16)
    padded = jnp.concatenate([normed, jnp.zeros((1, model_width), jnp.bfloat16)], axis=0)
    route_slot = route_slots(expert_ids, expert_count, capacity)
    token_table = jnp.full((expert_count * capacity,), token_count, jnp.int32)
    token_table = token_table.at[route_slot].set(
        jnp.arange(token_count * top_count, dtype=jnp.int32) // top_count
    )
    outgoing = padded[token_table].reshape(groups, local_experts, capacity, model_width)
    received = lax.all_to_all(outgoing, "expert", split_axis=0, concat_axis=0, tiled=True)
    gate_proj = jnp.einsum("secd,edf->secf", received, w_gate, preferred_element_type=jnp.float32)
    up_proj = jnp.einsum("secd,edf->secf", received, w_up, preferred_element_type=jnp.float32)
    hidden = (jax.nn.silu(gate_proj) * up_proj).astype(jnp.bfloat16)
    expert_out = jnp.einsum(
        "secf,efd->secd", hidden, w_down, preferred_element_type=jnp.float32
    ).astype(jnp.bfloat16)
    route_share = route_weights / jnp.sum(route_weights, axis=1, keepdims=True)
    returned = lax.all_to_all(expert_out, "expert", split_axis=0, concat_axis=0, tiled=True)
    picked = returned.reshape(expert_count * capacity, model_width)[route_slot].reshape(
        token_count, top_count, model_width
    )
    partial_value = jnp.sum(route_share[:, :, None] * picked.astype(jnp.float32), axis=1)
    mixed = lax.psum_scatter(
        partial_value.astype(jnp.bfloat16), "tensor", scatter_dimension=0, tiled=True
    )
    local_rows = source_rows - group_index * token_count
    group_hidden = lax.all_gather(mixed, "tensor", axis=0, tiled=True)
    handed = jnp.dot(
        group_hidden[local_rows], w_handover, preferred_element_type=jnp.float32
    ).astype(jnp.bfloat16)
    talker_in = handed.astype(jnp.float32) + codec_embeds.astype(jnp.float32)
    talker_normed = rms_scale(talker_in, talker_gain).astype(jnp.bfloat16)
    queries = jnp.dot(talker_normed, w_query, preferred_element_type=jnp.float32)
    key_value = jnp.dot(talker_normed, w_kv, preferred_element_type=jnp.float32)
    frame_count = talker_normed.shape[0]
    group_size = HEADS // KV_HEADS
    query_heads = rms_scale(
        queries.reshape(frame_count, KV_HEADS, group_size, HEAD), qk_gains[0]
    ).astype(jnp.bfloat16)
    key_heads = rms_scale(
        key_value[:, : KV_HEADS * HEAD].reshape(frame_count, KV_HEADS, HEAD), qk_gains[1]
    ).astype(jnp.bfloat16)
    key_heads = key_heads.reshape(frame_count, KV_HEADS * HEAD)
    value_heads = key_value[:, KV_HEADS * HEAD :].astype(jnp.bfloat16)
    group_keys, group_values = (
        lax.all_gather(key_heads, "tensor", axis=0, tiled=True),
        lax.all_gather(value_heads, "tensor", axis=0, tiled=True),
    )
    group_frames = frame_count * tensor_count
    key_positions = jnp.arange(group_frames, dtype=jnp.int32)
    query_positions = tensor_index * frame_count + jnp.arange(frame_count, dtype=jnp.int32)
    first_length = frame_lengths[0]
    same_dialog = (query_positions[:, None] >= first_length) == (
        key_positions[None, :] >= first_length
    )
    allowed = same_dialog & (key_positions[None, :] <= query_positions[:, None])
    scores = jnp.einsum(
        "fgrh,kgh->grfk",
        query_heads,
        group_keys.reshape(group_frames, KV_HEADS, HEAD),
        preferred_element_type=jnp.float32,
    ) * HEAD ** (-0.5)
    masked = jnp.where(allowed[None, None], scores, -jnp.inf)
    row_peak = jnp.max(masked, axis=-1, keepdims=True)
    exp_weights = jnp.exp(masked - row_peak).astype(jnp.bfloat16)
    denominator = jnp.sum(exp_weights.astype(jnp.float32), axis=-1)
    attended = jnp.einsum(
        "grfk,kgh->fgrh",
        exp_weights,
        group_values.reshape(group_frames, KV_HEADS, HEAD),
        preferred_element_type=jnp.float32,
    )
    attended = (
        (attended / jnp.transpose(denominator, (2, 0, 1))[..., None])
        .astype(jnp.bfloat16)
        .reshape(frame_count, HEADS * HEAD)
    )
    talker_out = jnp.dot(attended, w_out, preferred_element_type=jnp.float32).astype(jnp.bfloat16)
    return (mixed, talker_out)


def solution(mesh):
    placed = (
        P("expert", None),
        P(),
        P("expert", None),
        P("expert", None),
        P("expert", None, "tensor"),
        P("expert", None, "tensor"),
        P("expert", "tensor", None),
        P(("expert", "tensor"), None),
        P("expert"),
        P(("expert", "tensor")),
        P(),
        P(),
        P(),
        P(),
        P(),
        P(),
    )
    return jax.shard_map(
        per_device,
        mesh=mesh,
        in_specs=placed,
        out_specs=(P(("expert", "tensor"), None), P(("expert", "tensor"), None)),
        check_vma=False,
    )
```

profile of v0, /device:TPU:0, one launch (start us, length us, event | category | flops | bytes accessed | tf_op | source)
XLA Modules:
  0.0 934.8 jit_solution(7599500331344700635)
XLA Ops:
  7.2 1.0 copy.70
  8.2 0.1 eq.46
  8.3 0.1 eq.42
  8.5 0.7 broadcast_multiply_fusion
  9.2 0.1 copy.72
  9.3 0.6 fusion.24
  9.9 1.3 copy-done.2
  11.3 0.1 reduce-window.9
  11.3 1.8 broadcast_add_fusion
  13.2 2.6 copy.73
  15.7 0.1 copy.69
  15.9 0.2 mul.148
  16.0 2.5 fusion.23
  18.6 15.5 %scatter_custom_fusion = s32[4352]{0:T(1024)S(1)} fusion(s32[4096]{0:T(1024)S(1)} %bitcast.104, s32[4096]{0:T(1024)S(1)} %add_select_fusion, s32[]{:T(128)} %constant.26.clone.1), kind=kCustom, calls=%fused_computation.73 | custom fusion | bytes 17412 | tf_op jit(solution)/shard_map/scatter | solution.py:61
  34.2 2.1 fusion.10
  36.3 2.1 fusion.12
  38.4 1.5 concatenate.3
  39.9 35.1 %gather_fusion = bf16[4352,2048]{1,0:T(8,128)(2,1)} fusion(bf16[513,2048]{1,0:T(8,128)(2,1)} %concatenate.3, s32[5120]{0:T(1024)S(1)} %pad_clamp_fusion), kind=kCustom, calls=%fused_computation | custom fusion | bytes 35668992 | tf_op jit(solution)/shard_map/gather | solution.py:64
  75.0 25.2 %reshape.177 = bf16[32,4,34,2048]{3,2,1,0:T(8,128)(2,1)} reshape(bf16[4352,2048]{1,0:T(8,128)(2,1)} %gather_fusion) | data formatting | bytes 35651584 | tf_op jit(solution)/shard_map/reshape | solution.py:64
  100.2 21.1 %copy.74 = bf16[32,4,34,2048]{3,1,2,0:T(4,128)(2,1)} copy(bf16[32,4,34,2048]{3,2,1,0:T(8,128)(2,1)} %reshape.177) | data formatting | bytes 35651584 | tf_op jit(solution)/shard_map/reshape | solution.py:64
  121.3 205.4 %all_to_all.10 = bf16[32,4,34,2048]{3,1,2,0:T(4,128)(2,1)} all-to-all(bf16[32,4,34,2048]{3,1,2,0:T(4,128)(2,1)} %copy.74), channel_id=1, replica_groups=mesh['expert'=32,'tensor'=4] {'expert'}, dimensions={0} | all-to-all | bytes 35651584 | tf_op jit(solution)/shard_map/all_to_all | solution.py:65
  326.7 21.5 %fusion.1 = f32[4,32,34,192]{3,2,1,0:T(8,128)} fusion(bf16[32,4,34,2048]{3,1,2,0:T(4,128)(2,1)} %all_to_all.10, bf16[4,2048,192]{1,2,0:T(8,128)(2,1)S(1)} %copy-done.11), kind=kOutput, calls=%fused_computation.7 | convolution fusion | flops 3422552064 | bytes 24313856 | tf_op jit(solution)/shard_map/secd,edf->secf/dot_general | solution.py:67
  348.3 28.9 %convert_bitcast_fusion = bf16[32,4,34,2048]{3,2,0,1:T(8,128)(2,1)} fusion(f32[4,32,34,192]{3,2,1,0:T(8,128)} %fusion.1, bf16[32,4,34,2048]{3,1,2,0:T(4,128)(2,1)} %all_to_all.10, bf16[4,192,2048]{2,1,0:T(8,128)(2,1)S(1)} %copy-done, bf16[4,2048,192]{1,2,0:T(8,128)(2,1)} %param.20), kind=kOutput, calls=%fused_computation.6 | convolution fusion | flops 6859030528 | bytes 45285376 | tf_op jit(solution)/shard_map/secf,efd->secd/dot_general | solution.py:69
  377.1 21.2 %copy.77 = bf16[32,4,34,2048]{3,1,2,0:T(4,128)(2,1)} copy(bf16[32,4,34,2048]{3,2,0,1:T(8,128)(2,1)} %convert_bitcast_fusion) | data formatting | bytes 35651584 | tf_op jit(solution)/shard_map/convert_element_type | solution.py:71
  398.3 5.3 all-to-all-start.1
  403.6 0.0 reduce-scatter.2.cloned.1.call-start
  403.7 0.1 copy.68
  403.9 255.8 %all-to-all-done.1 = bf16[32,4,34,2048]{3,1,2,0:T(4,128)(2,1)} async-done(((bf16[32,4,34,2048]{3,1,2,0:T(4,128)(2,1)}), bf16[32,4,34,2048]{3,1,2,0:T(4,128)(2,1)}, u32[]{:S(2)}, u32[]{:S(2)}) %all-to-all-start.1) | async-done | bytes 17825824 | tf_op jit(solution)/shard_map/all_to_all | solution.py:73
  659.7 22.5 %copy.78 = bf16[32,4,34,2048]{3,2,1,0:T(8,128)(2,1)} copy(bf16[32,4,34,2048]{3,1,2,0:T(4,128)(2,1)} %all-to-all-done.1) | data formatting | bytes 35651584 | tf_op jit(solution)/shard_map/all_to_all | solution.py:73
  682.2 25.5 %reshape.178 = bf16[4352,2048]{1,0:T(8,128)(2,1)} reshape(bf16[32,4,34,2048]{3,2,1,0:T(8,128)(2,1)} %copy.78) | data formatting | bytes 35651584 | tf_op jit(solution)/shard_map/reshape | solution.py:74
  707.6 39.7 %gather_fusion.1 = bf16[4096,2048]{1,0:T(8,128)(2,1)} fusion(bf16[4352,2048]{1,0:T(8,128)(2,1)} %reshape.178, s32[4096]{0:T(1024)S(1)} %broadcast_clamp_fusion), kind=kCustom, calls=%fused_computation.1 | custom fusion | bytes 33570816 | tf_op jit(solution)/shard_map/gather | solution.py:74
  747.3 16.3 %fusion = bf16[512,2048]{1,0:T(8,128)(2,1)} fusion(bf16[4096,2048]{1,0:T(8,128)(2,1)} %gather_fusion.1, f32[512,8]{1,0:T(8,128)S(1)} %copy.68), kind=kLoop, calls=%fused_computation.5 | loop fusion | flops 24117248 | bytes 18890752 | tf_op jit(solution)/shard_map/reduce_sum | solution.py:77
  763.6 0.0 reduce-scatter.2.cloned.1.call-update
  763.6 0.0 all-gather.4.cloned.1.call-start
  763.7 60.4 %reduce-scatter.2.cloned.1.call-done = bf16[128,2048]{1,0:T(8,128)(2,1)} async-done(((bf16[512,2048]{1,0:T(8,128)(2,1)}), bf16[128,2048]{1,0:T(8,128)(2,1)}) %reduce-scatter.2.cloned.1.call-update) | async-done | bytes 524304 | tf_op jit(solution)/shard_map/reduce_scatter | solution.py:78
  824.1 0.0 all-gather.4.cloned.1.call-update
  824.1 0.0 all-gather.8.cloned.1.call-start
  824.2 32.8 %all-gather.4.cloned.1.call-done = bf16[512,2048]{1,0:T(8,128)(2,1)} async-done(((bf16[128,2048]{1,0:T(8,128)(2,1)}), bf16[512,2048]{1,0:T(8,128)(2,1)}) %all-gather.4.cloned.1.call-update) | async-done | bytes 2097168 | tf_op jit(solution)/shard_map/all_gather | solution.py:82
  857.0 4.2 gather_fusion.2
  861.3 3.7 multiply_reduce_fusion.1
  865.0 0.8 fusion.44
  865.8 0.2 mul.161
  866.0 0.3 reduce_sum.80
  866.4 0.3 mul.162
  866.7 0.8 fusion.35
  867.6 0.2 all-gather.6.cloned.1.call-start
  867.9 0.3 fusion.33
  868.2 0.7 slice.45
  868.9 2.3 fusion.43
  871.3 0.9 reshape.181
  872.2 1.6 multiply_reduce_fusion
  873.8 0.2 copy.81
  874.0 0.3 copy.82
  874.3 0.0 all-gather.6.cloned.1.call-update
  874.3 1.6 multiply_convert_fusion
  875.9 15.9 %all-gather.8.cloned.1.call-done = bf16[1024,512]{1,0:T(8,128)(2,1)} async-done(((bf16[256,512]{1,0:T(8,128)(2,1)}), bf16[1024,512]{1,0:T(8,128)(2,1)}) %all-gather.8.cloned.1.call-update) | async-done | bytes 1048592 | tf_op jit(solution)/shard_map/all_gather | solution.py:101
  891.8 1.3 reshape.180
  893.1 1.4 fusion.5
  894.5 3.2 copy-done.3
  897.8 1.7 convert_reduce_fusion
  899.5 18.8 %all-gather.6.cloned.1.call-done = bf16[1024,512]{1,0:T(8,128)(2,1)} async-done(((bf16[256,512]{1,0:T(8,128)(2,1)}), bf16[1024,512]{1,0:T(8,128)(2,1)}) %all-gather.6.cloned.1.call-update) | async-done | bytes 1048592 | tf_op jit(solution)/shard_map/all_gather | solution.py:102
  918.3 2.3 copy.93
  920.5 6.0 fusion.27
  926.5 1.5 convolution_convert_fusion
  (48 shorter events, 0.4 us)
Async XLA Ops:
  7.2 341.1 %copy-start = (bf16[4,192,2048]{2,1,0:T(8,128)(2,1)S(1)}, bf16[4,192,2048]{2,1,0:T(8,128)(2,1)}, u32[]{:S(2)}) copy-start(bf16[4,192,2048]{2,1,0:T(8,128)(2,1)} %param.22) | copy-start | bytes 9437188
  9.9 1.4 copy-start.2
  13.2 23.1 %copy-start.8 = (f32[2048]{0:T(1024)S(1)}, f32[2048]{0:T(1024)}, u32[]{:S(2)}) copy-start(f32[2048]{0:T(1024)} %param.17) | copy-start | bytes 24580
  121.3 205.5 %copy-start.11 = (bf16[4,2048,192]{1,2,0:T(8,128)(2,1)S(1)}, bf16[4,2048,192]{1,2,0:T(8,128)(2,1)}, u32[]{:S(2)}) copy-start(bf16[4,2048,192]{1,2,0:T(8,128)(2,1)} %param.21) | copy-start | bytes 9437188
  398.3 5.4 copy-start.7
  398.3 261.3 %all-to-all-start.1 = ((bf16[32,4,34,2048]{3,1,2,0:T(4,128)(2,1)}), bf16[32,4,34,2048]{3,1,2,0:T(4,128)(2,1)}, u32[]{:S(2)}, u32[]{:S(2)}) async-start(bf16[32,4,34,2048]{3,1,2,0:T(4,128)(2,1)} %copy.77), calls=%async_computation.1 | async-start | bytes 35651584 | tf_op jit(solution)/shard_map/all_to_all | solution.py:73
  403.6 420.4 %reduce-scatter.2.cloned.1.call-start = ((), (), s32[]{:S(2)}) async-start(), calls=%async_computation.3 | async-start | bytes 2621440 | tf_op jit(solution)/shard_map/reduce_scatter | solution.py:78
  747.3 76.8 %copy-start.9 = (s32[256]{0:T(256)S(1)}, s32[256]{0:T(256)}, u32[]{:S(2)}) copy-start(s32[256]{0:T(256)} %param.25) | copy-start | bytes 3076
  747.3 76.9 %copy-start.10 = (f32[2,128]{1,0:T(2,128)S(1)}, f32[2,128]{1,0:T(2,128)}, u32[]{:S(2)}) copy-start(f32[2,128]{1,0:T(2,128)} %param.30) | copy-start | bytes 3076
  763.6 93.4 %all-gather.4.cloned.1.call-start = ((), (), s32[]{:S(2)}) async-start(), calls=%async_computation.4 | async-start | bytes 2621440 | tf_op jit(solution)/shard_map/all_gather | solution.py:82
  824.1 67.7 %all-gather.8.cloned.1.call-start = ((), (), s32[]{:S(2)}) async-start(), calls=%async_computation.6 | async-start | bytes 1310720 | tf_op jit(solution)/shard_map/all_gather | solution.py:101
  824.2 37.0 %copy-start.12 = (bf16[256,1024]{1,0:T(8,128)(2,1)S(1)}, bf16[256,1024]{1,0:T(8,128)(2,1)}, u32[]{:S(2)}) copy-start(bf16[256,1024]{1,0:T(8,128)(2,1)} %param.23) | copy-start | bytes 1572868
  861.3 3.7 copy-start.4
  861.3 3.7 copy-start.6
  865.0 2.8 copy-start.13
  867.6 50.7 %all-gather.6.cloned.1.call-start = ((), (), s32[]{:S(2)}) async-start(), calls=%async_computation.5 | async-start | bytes 1310720 | tf_op jit(solution)/shard_map/all_gather | solution.py:102
  894.5 3.2 copy-start.3
  920.5 6.0 copy-start.5
  920.5 7.5 copy-start.1
Sparse Core Ops, SparseCore 0:
  763.7 60.2 reduce-scatter.1
  826.4 30.5 all-gather.3
  867.7 23.9 all-gather.7
  894.0 24.2 all-gather.5
where the time goes:
time: 944 us; the launch traced here: 935 us
  waiting for transfers between devices  384 us (41%)
  local copies, waits for them, and re-layouts  227 us (24%)
  blocking collectives  205 us (22%)
  matrix products  66.1 us (7%)
  other arithmetic  32.8 us (3%)
  between operations  14.4 us (2%)
    all_to_all x1, waiting for transfers between devices, per_device(): lax.all_to_all(expert_out, 'expert', split_axis=0, concat_axis=0, tiled=T...  256 us
    all_to_all x1, blocking collectives, per_device(): lax.all_to_all(outgoing, 'expert', split_axis=0, concat_axis=0, tiled=True)  205 us
    reduce_scatter x1, waiting for transfers between devices, per_device(): lax.psum_scatter(partial_value.astype(jnp.bfloat16), 'tensor', scatter_di...  60.4 us
    reshape x2, local copies, waits for them, and re-layouts, per_device(): padded[token_table].reshape(groups, local_experts, capacity, model_width)  46.3 us
    gather x1, local copies, waits for them, and re-layouts, per_device(): returned.reshape(expert_count * capacity, model_width)[route_slot]  39.7 us
    gather x1, local copies, waits for them, and re-layouts, per_device(): padded[token_table].reshape(groups, local_experts, capacity, model_width)  35.1 us
    all_gather x1, waiting for transfers between devices, per_device(): group_hidden = lax.all_gather(mixed, 'tensor', axis=0, tiled=True)  32.8 us
    dot_general x1, matrix products, per_device(): jnp.einsum('secf,efd->secd', hidden, w_down, preferred_element_type=jnp.f...  28.9 us
  transfers between devices with their start and end apart: 5, of which 5 were waited for; matrix products, arithmetic and copies ran while one was open for 1% of the time, Pallas kernels for 0%

commit v1 on v0

v1 whole, which is shorter than its diff:
```python
import functools

import jax
import jax.numpy as jnp
from jax import lax
from jax.experimental import pallas as pl
from jax.experimental.pallas import tpu as pltpu
from jax.sharding import PartitionSpec as P

MESH = pl.DeviceIdType.MESH
BF = jnp.bfloat16
F32 = jnp.float32
EPS = 1e-06
GROUPS = 32
SLOT = 32
CHUNKS = 4
CW = 512


def peer_shifts():
    def opposite(s):
        return ((4 - s[0]) % 4, (4 - s[1]) % 4, s[2])

    every = [
        (dx, dz, dc)
        for dx in range(4)
        for dz in range(4)
        for dc in range(2)
        if (dx, dz, dc) != (0, 0, 0)
    ]
    order, seen = [], set()
    for s in sorted(every, key=lambda s: (sum(min(v, 4 - v) for v in s[:2]), s)):
        for one in (s, opposite(s)):
            if one not in seen:
                seen.add(one)
                order.append(one)
    return order[::-1]


SHIFTS = peer_shifts()
REMOTE = len(SHIFTS)


def mm(a, b):
    return jnp.dot(a, b, preferred_element_type=F32)


def mm_nt(a, b):
    return lax.dot_general(a, b, (((1,), (1,)), ((), ())), preferred_element_type=F32)


def iota(shape, dim):
    return lax.broadcasted_iota(jnp.int32, shape, dim)


def ones_where(cond):
    return jnp.where(cond, 1.0, 0.0).astype(BF)


def rms(v, gain):
    return v * lax.rsqrt(jnp.mean(v * v, axis=-1, keepdims=True) + EPS) * gain


def kernel(
    tok_hbm, gain, ids, rw, wg_hbm, wu_hbm, wd_hbm, codec_hbm, flen, src, wh_hbm, tgain, wq_hbm, wkv_hbm, qkg, wo_hbm,
    thinker, talker,
    tok, wg, wu, wd, wh, wq, wkv, wo, pw, sel, sb, xb, hb, rb, rem_s, rem_r, orem, rrem, ps, pr,
    hacc, ha, codec, srcs, oh, tn, kb, vb, bias, qb, at, acc_o,
    own_sem, wsend, wrecv, dsend, drecv, rsend, rrecv, psend, precv, hsend, hrecv, csend, crecv, ssend, srecv,
):
    e = lax.axis_index("expert")
    t = lax.axis_index("tensor")
    x, z, c = e // 8, (e // 2) % 4, e % 2

    def shifted(s, sign):
        return (
            lax.rem(x + sign * s[0] + 4, 4) * 8
            + lax.rem(z + sign * s[1] + 4, 4) * 2
            + lax.rem(c + s[2], 2)
        )

    to = [shifted(s, 1) for s in SHIFTS]
    back = [shifted(s, -1) for s in SHIFTS]
    side = [t] + [lax.rem(t + d, 4) for d in (1, 2, 3)]

    barrier = pltpu.get_barrier_semaphore()
    for j in to:
        pl.semaphore_signal(barrier, inc=1, device_id=(j, t), device_id_type=MESH)
    for d in (1, 2, 3):
        pl.semaphore_signal(barrier, inc=1, device_id=(e, side[d]), device_id_type=MESH)

    local = [
        pltpu.make_async_copy(tok_hbm, tok, own_sem.at[0]),
        pltpu.make_async_copy(wg_hbm.at[t], wg.at[0], own_sem.at[1]),
        pltpu.make_async_copy(wu_hbm.at[t], wu.at[0], own_sem.at[2]),
        pltpu.make_async_copy(wd_hbm.at[t], wd.at[0], own_sem.at[3]),
        pltpu.make_async_copy(wh_hbm, wh, own_sem.at[4]),
        pltpu.make_async_copy(wkv_hbm, wkv, own_sem.at[5]),
        pltpu.make_async_copy(wq_hbm, wq, own_sem.at[6]),
        pltpu.make_async_copy(wo_hbm, wo, own_sem.at[7]),
        pltpu.make_async_copy(codec_hbm, codec.at[t], own_sem.at[8]),
    ]
    for cp in local:
        cp.start()

    def remote(a, b, s, r, device):
        return pltpu.make_async_remote_copy(
            src_ref=a, dst_ref=b, send_sem=s, recv_sem=r, device_id=device, device_id_type=MESH
        )

    pl.semaphore_wait(barrier, REMOTE + 3)

    gate_up = {}
    for d in (1, 3, 2):
        for a, (h, v) in enumerate(((wg_hbm, wg), (wu_hbm, wu))):
            gate_up[a, d] = remote(h.at[side[d]], v.at[d], wsend.at[a, d], wrecv.at[a, d], (e, side[d]))
            gate_up[a, d].start()
    source_copies = [remote(src, srcs.at[t], ssend.at[d], srecv.at[d], (e, side[d])) for d in (1, 2, 3)]
    for cp in source_copies:
        cp.start()
    srcs[t] = src[...]

    slot_row = iota((GROUPS, 512), 0)
    wanted = jnp.full((GROUPS, 512), 4 * e + t, jnp.int32)
    for i in range(REMOTE):
        wanted = jnp.where(slot_row == i, 4 * to[i] + t, wanted)
    total = jnp.sum(rw[...], axis=0, keepdims=True)
    share = rw[...] / total
    chosen = jnp.zeros((GROUPS, 512), F32)
    weight = jnp.zeros((GROUPS, 512), F32)
    for k in range(8):
        hit = ids[k : k + 1, :] == wanted
        chosen = chosen + jnp.where(hit, 1.0, 0.0)
        weight = weight + jnp.where(hit, share[k : k + 1, :], 0.0)
    upper = ones_where(iota((512, 512), 0) < iota((512, 512), 1))
    rank = mm(chosen.astype(BF), upper)
    rank = jnp.where(chosen > 0.5, rank, -1.0).astype(BF)
    weight = weight.astype(BF)

    local[0].wait()

    def norm_tile(i, carry):
        rows = pl.ds(pl.multiple_of(i * 64, 64), 64)
        tok[rows, :] = rms(tok[rows, :].astype(F32), gain[...]).astype(BF)
        return carry

    lax.fori_loop(0, 8, norm_tile, 0)

    def dispatch_tile(i, carry):
        rows = pl.ds(pl.multiple_of(i * 128, 128), 128)
        spread = ones_where(((iota((128, GROUPS), 0) + i * 128) >> 5) == iota((128, GROUPS), 1))
        place = (iota((128, 512), 0) & 31).astype(F32)
        hit = mm(spread, rank) == place
        pw[rows, :] = jnp.where(hit, mm(spread, weight), 0.0).astype(BF)
        sb[rows, :] = mm(ones_where(hit), tok[...]).astype(BF)
        return carry

    lax.fori_loop(0, 8, dispatch_tile, 0)
    dispatch = []
    for i in range(REMOTE):
        cp = remote(
            sb.at[pl.ds(i * SLOT, SLOT)], xb.at[pl.ds(i * SLOT, SLOT)], dsend.at[0], drecv.at[0], (to[i], t)
        )
        cp.start()

    spread = ones_where((iota((64, GROUPS), 0) >> 1) == iota((64, GROUPS), 1))
    place = (iota((64, 512), 0) & 1).astype(F32) + 32.0
    hit = mm(spread, rank) == place
    pw[1024:1088, :] = jnp.where(hit, mm(spread, weight), 0.0).astype(BF)
    extra = mm(ones_where(hit), tok[...]).astype(BF)
    row, col = iota((512, 64), 0), iota((512, 64), 1)
    same = ((row >> 4) == (col >> 1)) & ((row & 1) == (col & 1))
    packed = jnp.zeros((512, 256), F32)
    for q in range(8):
        packed = packed + mm(ones_where(same & (((row >> 1) & 7) == q)), extra[:, q * 256 : (q + 1) * 256])
    rem_s[...] = packed.astype(BF)
    for i in range(REMOTE):
        cp = remote(rem_s.at[pl.ds(i * 16, 16)], rem_r.at[pl.ds(i * 16, 16)], dsend.at[1], drecv.at[1], (to[i], t))
        cp.start()
    xb[REMOTE * SLOT : 1024, :] = sb[REMOTE * SLOT : 1024, :]
    rem_r[REMOTE * 16 : 512, :] = rem_s[REMOTE * 16 : 512, :]

    eye = ones_where(iota((512, 512), 0) == iota((512, 512), 1))

    def flip_tile(i, carry):
        part = pl.ds(pl.multiple_of(i * 256, 256), 256)
        sel[:, part] = mm_nt(eye, pw[part, :]).astype(BF)
        return carry

    lax.fori_loop(0, 4, flip_tile, 0)
    sel[:, 1024:1088] = mm_nt(eye, pw[1024:1088, :]).astype(BF)

    kb[...] = jnp.zeros_like(kb)
    for g in range(4):
        vb[:, g * 256 : g * 256 + 128] = jnp.zeros((1024, 128), BF)
        vb[:, g * 256 + 128 : g * 256 + 256] = jnp.ones((1024, 128), BF)
    first = flen[0]
    q_pos = iota((256, 1024), 0) + t * 256
    k_pos = iota((256, 1024), 1)
    q_late = jnp.where(q_pos >= first, 1, 0)
    k_late = jnp.where(k_pos >= first, 1, 0)
    bias[...] = jnp.where((q_late == k_late) & (k_pos <= q_pos), 0.0, -1e30)

    for d in (1, 2, 3):
        source_copies[d - 1].wait()
    eye256 = ones_where(iota((256, 256), 0) == iota((256, 256), 1))

    def pick_tile(b, carry):
        want = srcs[b] - e * 512
        oh[b] = mm_nt(eye256, ones_where(iota((512, 256), 0) == want)).astype(BF)
        return carry

    lax.fori_loop(0, 4, pick_tile, 0)

    remote(xb.at[pl.ds(0, REMOTE * SLOT)], xb.at[pl.ds(0, REMOTE * SLOT)], dsend.at[0], drecv.at[0], (to[0], t)).wait()
    remote(rem_r.at[pl.ds(0, REMOTE * 16)], rem_r.at[pl.ds(0, REMOTE * 16)], dsend.at[1], drecv.at[1], (to[0], t)).wait()
    down = {}
    for k in range(CHUNKS):
        cols = pl.ds(k * CW, CW)
        for d in (1, 3, 2):
            down[k, d] = remote(
                wd_hbm.at[side[d], :, cols], wd.at[d, :, cols], wsend.at[2 + k, d], wrecv.at[2 + k, d], (e, side[d])
            )
            down[k, d].start()
    row, col = iota((64, 512), 0), iota((64, 512), 1)
    same = ((col >> 4) == (row >> 1)) & ((row & 1) == (col & 1))
    for q in range(8):
        xb[1024:1088, q * 256 : (q + 1) * 256] = mm(
            ones_where(same & (((col >> 1) & 7) == q)), rem_r[...]
        ).astype(BF)

    for d in (0, 1, 3, 2):
        if d == 0:
            local[1].wait()
            local[2].wait()
        else:
            gate_up[0, d].wait()
            gate_up[1, d].wait()

        def hidden_tile(i, carry, d=d):
            rows = pl.ds(pl.multiple_of(i * 272, 16), 272)
            g = mm_nt(xb[rows, :], wg[d])
            u = mm_nt(xb[rows, :], wu[d])
            hb[d, rows, :] = (g / (1.0 + jnp.exp(-g)) * u).astype(BF)
            return carry

        lax.fori_loop(0, 4, hidden_tile, 0)

    local[3].wait()
    row, col = iota((256, 64), 0), iota((256, 64), 1)
    pack = [
        ones_where(((row >> 3) == (col >> 1)) & ((row & 1) == (col & 1)) & (((row >> 1) & 3) == q)) for q in range(4)
    ]
    row, col = iota((64, 256), 0), iota((64, 256), 1)
    unpack = [
        ones_where(((col >> 3) == (row >> 1)) & ((row & 1) == (col & 1)) & (((col >> 1) & 3) == q)) for q in range(4)
    ]
    for k in range(CHUNKS):
        cols = pl.ds(k * CW, CW)
        for d in (1, 3, 2):
            down[k, d].wait()

        def out_tile(i, carry, cols=cols):
            rows = pl.ds(pl.multiple_of(i * 272, 16), 272)
            o = mm(hb[0, rows, :], wd[0, :, cols])
            for d in (1, 3, 2):
                o = o + mm(hb[d, rows, :], wd[d, :, cols])
            sb[rows, cols] = o.astype(BF)
            return carry

        lax.fori_loop(0, 4, out_tile, 0)
        for i in range(REMOTE):
            cp = remote(
                sb.at[pl.ds(i * SLOT, SLOT), cols], rb.at[pl.ds(i * SLOT, SLOT), cols],
                rsend.at[0, k], rrecv.at[0, k], (back[i], t),
            )
            cp.start()
        last = sb[1024:1088, cols]
        packed = jnp.zeros((256, 128), F32)
        for q in range(4):
            packed = packed + mm(pack[q], last[:, q * 128 : (q + 1) * 128])
        orem[k] = packed
        for i in range(REMOTE):
            cp = remote(
                orem.at[k, pl.ds(i * 8, 8)], rrem.at[k, pl.ds(i * 8, 8)],
                rsend.at[1, k], rrecv.at[1, k], (back[i], t),
            )
            cp.start()
        rb[REMOTE * SLOT : 1024, cols] = sb[REMOTE * SLOT : 1024, cols]
        rrem[k, REMOTE * 8 : 256, :] = orem[k, REMOTE * 8 : 256, :]

    local[8].wait()
    for d in (1, 2, 3):

        @pl.when(t + d < 4)
        def _(d=d):
            remote(codec.at[t], codec.at[t], csend.at[d], crecv.at[d], (e, side[d])).start()

    local[4].wait()
    sums = {}
    own = pl.ds(pl.multiple_of(t * 128, 128), 128)
    hacc[...] = jnp.zeros_like(hacc)

    def finish_chunk(k):
        cols = pl.ds(k * CW, CW)
        total = ps[own, cols].astype(F32)
        for d in (1, 2, 3):
            sums[k, d].wait()
            total = total + pr[d, :, cols].astype(F32)
        done = total.astype(BF)
        thinker[:, cols] = done
        hacc[...] += mm(done, wh[cols, :])

    for k in range(CHUNKS):
        cols = pl.ds(k * CW, CW)
        remote(
            sb.at[pl.ds(0, REMOTE * SLOT), cols], rb.at[pl.ds(0, REMOTE * SLOT), cols],
            rsend.at[0, k], rrecv.at[0, k], (to[0], t),
        ).wait()
        remote(
            orem.at[k, pl.ds(0, REMOTE * 8)], rrem.at[k, pl.ds(0, REMOTE * 8)],
            rsend.at[1, k], rrecv.at[1, k], (to[0], t),
        ).wait()
        got = rrem[k].astype(BF)
        for q in range(4):
            rb[1024:1088, k * CW + q * 128 : k * CW + (q + 1) * 128] = mm(unpack[q], got).astype(BF)

        def sum_tile(i, carry, cols=cols):
            rows = pl.ds(pl.multiple_of(i * 128, 128), 128)
            ps[rows, cols] = mm(sel[rows, :], rb[:, cols]).astype(BF)
            return carry

        lax.fori_loop(0, 4, sum_tile, 0)
        for d in (1, 2, 3):
            rows = pl.ds(pl.multiple_of(side[d] * 128, 128), 128)
            sums[k, d] = remote(ps.at[rows, cols], pr.at[d, :, cols], psend.at[k, d], precv.at[k, d], (e, side[d]))
            sums[k, d].start()
        if k > 0:
            finish_chunk(k - 1)
    finish_chunk(CHUNKS - 1)
    ha[own, :] = hacc[...].astype(BF)
    handed = [remote(ha.at[own], ha.at[own], hsend.at[d], hrecv.at[d], (e, side[d])) for d in (1, 2, 3)]
    for cp in handed:
        cp.start()
    for d in (1, 2, 3):

        @pl.when(t + d < 4)
        def _(d=d):
            remote(codec.at[t], codec.at[t], csend.at[d], crecv.at[d], (e, side[d])).wait_send()

        @pl.when(t >= d)
        def _(d=d):
            remote(codec.at[t - d], codec.at[t - d], csend.at[d], crecv.at[d], (e, side[d])).wait_recv()

    for i in (5, 6, 7):
        local[i].wait()
    for cp in handed:
        cp.wait()

    def frame_tile(b, carry):
        rows = pl.ds(pl.multiple_of(b * 256, 256), 256)
        v = mm(oh[b], ha[...]) + codec[b].astype(F32)
        n = rms(v, tgain[...]).astype(BF)
        tn[rows, :] = n
        kv = mm(n, wkv[...])
        for g in range(4):
            kb[rows, g * 128 : (g + 1) * 128] = rms(kv[:, g * 128 : (g + 1) * 128], qkg[1:2, :]).astype(BF)
            vb[rows, g * 256 : g * 256 + 128] = kv[:, 512 + g * 128 : 640 + g * 128].astype(BF)
        return carry

    lax.fori_loop(0, t + 1, frame_tile, 0)
    mine = pl.ds(pl.multiple_of(t * 256, 256), 256)
    queries = mm(tn[mine, :], wq[...])
    for h in range(8):
        qb[:, h * 128 : (h + 1) * 128] = rms(queries[:, h * 128 : (h + 1) * 128], qkg[0:1, :]).astype(BF)

    def head(h, carry):
        lanes = pl.ds(pl.multiple_of(h * 128, 128), 128)
        keys = kb[:, pl.ds(pl.multiple_of((h >> 1) * 128, 128), 128)]
        s = mm_nt(qb[:, lanes], keys) * (128.0 ** -0.5) + bias[...]
        w = jnp.exp(s - jnp.max(s, axis=-1, keepdims=True)).astype(BF)
        o = mm(w, vb[:, pl.ds(pl.multiple_of((h >> 1) * 256, 256), 256)])
        at[:, lanes] = (o[:, :128] / o[:, 128:]).astype(BF)
        return carry

    lax.fori_loop(0, 8, head, 0)
    talker[...] = mm(at[...], wo[...]).astype(BF)


def per_device(
    tokens, norm_gain, expert_ids, route_weights, w_gate, w_up, w_down, codec_embeds,
    frame_lengths, source_rows, w_handover, talker_gain, w_query, w_kv, qk_gains, w_out,
):
    vm = pl.BlockSpec(memory_space=pltpu.VMEM)
    hb = pl.BlockSpec(memory_space=pl.ANY)
    sm = pl.BlockSpec(memory_space=pltpu.SMEM)
    dma = pltpu.SemaphoreType.DMA
    scratch = [
        ((512, 2048), BF),
        ((4, 192, 2048), BF),
        ((4, 192, 2048), BF),
        ((4, 192, 2048), BF),
        ((2048, 1024), BF),
        ((1024, 1024), BF),
        ((1024, 1024), BF),
        ((1024, 1024), BF),
        ((1088, 512), BF),
        ((512, 1088), BF),
        ((1088, 2048), BF),
        ((1088, 2048), BF),
        ((4, 1088, 192), BF),
        ((1088, 2048), BF),
        ((512, 256), BF),
        ((512, 256), BF),
        ((4, 256, 128), F32),
        ((4, 256, 128), F32),
        ((512, 2048), BF),
        ((4, 128, 2048), BF),
        ((128, 1024), F32),
        ((512, 1024), BF),
        ((4, 256, 1024), BF),
        ((4, 1, 256), jnp.int32),
        ((4, 256, 512), BF),
        ((1024, 1024), BF),
        ((1024, 512), BF),
        ((1024, 1024), BF),
        ((256, 1024), F32),
        ((256, 1024), BF),
        ((256, 1024), BF),
        ((8, 128), F32),
    ]
    sems = [(9,), (6, 4), (6, 4), (2,), (2,), (2, 4), (2, 4), (4, 4), (4, 4), (4,), (4,), (4,), (4,), (4,), (4,)]
    return pl.pallas_call(
        kernel,
        out_shape=(
            jax.ShapeDtypeStruct((128, 2048), BF),
            jax.ShapeDtypeStruct((256, 1024), BF),
        ),
        in_specs=[hb, vm, vm, vm, hb, hb, hb, hb, sm, vm, hb, vm, hb, hb, vm, hb],
        out_specs=(vm, vm),
        scratch_shapes=[pltpu.VMEM(s, d) for s, d in scratch] + [dma(s) for s in sems],
        compiler_params=pltpu.CompilerParams(
            collective_id=0, has_side_effects=True, vmem_limit_bytes=61 << 20
        ),
        cost_estimate=pl.CostEstimate(flops=20_000_000_000, bytes_accessed=40_000_000, transcendentals=4_000_000),
        name="expert_talker",
    )(
        tokens,
        norm_gain.reshape(1, 2048),
        expert_ids.T,
        route_weights.T,
        jnp.swapaxes(w_gate, 1, 2),
        jnp.swapaxes(w_up, 1, 2),
        w_down,
        codec_embeds,
        frame_lengths,
        source_rows.reshape(1, 256),
        w_handover,
        talker_gain.reshape(1, 1024),
        w_query,
        w_kv,
        qk_gains,
        w_out,
    )


def solution(mesh):
    placed = (
        P("expert", None),
        P(),
        P("expert", None),
        P("expert", None),
        P("expert", None, "tensor"),
        P("expert", None, "tensor"),
        P("expert", "tensor", None),
        P(("expert", "tensor"), None),
        P("expert"),
        P(("expert", "tensor")),
        P(),
        P(),
        P(),
        P(),
        P(),
        P(),
    )
    return jax.shard_map(
        per_device,
        mesh=mesh,
        in_specs=placed,
        out_specs=(P(("expert", "tensor"), None), P(("expert", "tensor"), None)),
        check_vma=False,
    )
```

time: 944 us -> 197 us (0.21)
  waiting for transfers between devices: 384 us -> 0 us
  local copies, waits for them, and re-layouts: 227 us -> 3.75 us
  blocking collectives: 205 us -> 0 us
  Pallas kernels: 0 us -> 192 us
  matrix products: 66.1 us -> 0 us
  other arithmetic: 32.8 us -> 0 us
  between operations: 14.4 us -> 0.65 us
    all_to_all x1 -> x0, waiting for transfers between devices: 256 us -> none  [per_device(): lax.all_to_all(expert_out, 'expert', split_axis=0, concat_axis=0, tiled=T...]
    all_to_all x1 -> x0, blocking collectives: 205 us -> none  [per_device(): lax.all_to_all(outgoing, 'expert', split_axis=0, concat_axis=0, tiled=True)]
    pallas_call x0 -> x1, Pallas kernels: none -> 192 us  [per_device(): pl.pallas_call(kernel, out_shape=(jax.ShapeDtypeStruct((128, 2048), BF),...]
    gather x3 -> x0, local copies, waits for them, and re-layouts: 79 us -> none  [the longest x1 39.7 us: per_device(): returned.reshape(expert_count * capacity, model_width)[route_slot]]
    reshape x6 -> x0, local copies, waits for them, and re-layouts: 76.2 us -> none  [the longest x2 46.3 us: per_device(): padded[token_table].reshape(groups, local_experts, capacity, model_width)]
    all_gather x3 -> x0, waiting for transfers between devices: 67.4 us -> none  [the longest x1 32.8 us: per_device(): group_hidden = lax.all_gather(mixed, 'tensor', axis=0, tiled=True)]
    dot_general x8 -> x0, matrix products: 66.1 us -> none  [the longest x1 28.9 us: per_device(): jnp.einsum('secf,efd->secd', hidden, w_down, preferred_element_type=jnp.f...]
    reduce_scatter x1 -> x0, waiting for transfers between devices: 60.4 us -> none  [per_device(): lax.psum_scatter(partial_value.astype(jnp.bfloat16), 'tensor', scatter_di...]
  transfers between devices with their start and end apart: 5 -> 0, of which waited for: 5 -> 0; matrix products, arithmetic and copies ran while one was open for 1% -> 0% of each run, Pallas kernels for 0% -> 0%
where the time goes in v1:
time: 197 us
  Pallas kernels  192 us (97%)
  local copies, waits for them, and re-layouts  3.75 us (2%)
    pallas_call x1, Pallas kernels, per_device(): pl.pallas_call(kernel, out_shape=(jax.ShapeDtypeStruct((128, 2048), BF),...  192 us

profile of v1, /device:TPU:0, one launch (start us, length us, event | category | flops | bytes accessed | tf_op | source)
XLA Modules:
  0.0 196.9 jit_solution(1709276961903772544)
XLA Ops:
  0.6 192.5 %expert_talker.1 = (bf16[128,2048]{1,0:T(8,128)(2,1)}, bf16[256,1024]{1,0:T(8,128)(2,1)}) custom-call(bf16[512,2048]{1,0:T(8,128)(2,1)} %tok_hbm.1, f32[1,2048]{1,0:T(1,128)} %bitcast.11, s32[8,512]{1,0:T(8,128)} %bitcast.9, f32[8,512]{1,0:T(8,128)} %bitcast.10, bf16[4,192,2048]{2,1,0:T(8,128)(2,1)} %bitcast.7, bf16[4,192,2048]{2,1,0:T(8,128)(2,1)} %bitcast.8, ...), custom_call_target="tpu_custom_call" | custom-call | flops 20000000000 | bytes 40000000 | tf_op jit(solution)/shard_map/expert_talker/pallas_call | solution.py:433
  193.1 1.9 copy.20
  195.0 1.9 copy.21

commit v2 on v1

--- a/solution.py
+++ b/solution.py
@@ -1,4 +1,4 @@
-import functools
+import math
 
 import jax
 import jax.numpy as jnp
@@ -15,6 +15,9 @@
 SLOT = 32
 CHUNKS = 4
 CW = 512
+PIECES = ((0, 512, 0), (512, 512, 1), (1024, 512, 2), (1536, 256, 3), (1792, 256, None))
+PAIRED = 3
+STEP = (0, 1, 3, 2)
 
 
 def peer_shifts():
@@ -62,11 +65,11 @@
 
 
 def kernel(
-    tok_hbm, gain, ids, rw, wg_hbm, wu_hbm, wd_hbm, codec_hbm, flen, src, wh_hbm, tgain, wq_hbm, wkv_hbm, qkg, wo_hbm,
-    thinker, talker,
-    tok, wg, wu, wd, wh, wq, wkv, wo, pw, sel, sb, xb, hb, rb, rem_s, rem_r, orem, rrem, ps, pr,
-    hacc, ha, codec, srcs, oh, tn, kb, vb, bias, qb, at, acc_o,
-    own_sem, wsend, wrecv, dsend, drecv, rsend, rrecv, psend, precv, hsend, hrecv, csend, crecv, ssend, srecv,
+    tok_hbm, gain, ids, rw, wg_hbm, wu_hbm, wd_hbm, codec_hbm, flen, src, wh_hbm, tgain, wq_hbm, wkv_hbm, qkg,
+    thinker, at,
+    tok, wg, wu, wd, wh, wq, wkv, pw, sel, sb, xb, hb, rb, rem_s, rem_r, orem, rrem, ps, pr,
+    hacc, ha, codec, srcs, oh, tn, kb, vb, bias, qb,
+    own_sem, wsend, wrecv, dsend, drecv, rsend, rrecv, psend, precv, qsend, qrecv, hsend, hrecv, csend, crecv, ssend, srecv,
 ):
     e = lax.axis_index("expert")
     t = lax.axis_index("tensor")
@@ -97,8 +100,7 @@
         pltpu.make_async_copy(wh_hbm, wh, own_sem.at[4]),
         pltpu.make_async_copy(wkv_hbm, wkv, own_sem.at[5]),
         pltpu.make_async_copy(wq_hbm, wq, own_sem.at[6]),
-        pltpu.make_async_copy(wo_hbm, wo, own_sem.at[7]),
-        pltpu.make_async_copy(codec_hbm, codec.at[t], own_sem.at[8]),
+        pltpu.make_async_copy(codec_hbm, codec.at[t], own_sem.at[7]),
     ]
     for cp in local:
         cp.start()
@@ -107,18 +109,6 @@
         return pltpu.make_async_remote_copy(
             src_ref=a, dst_ref=b, send_sem=s, recv_sem=r, device_id=device, device_id_type=MESH
         )
-
-    pl.semaphore_wait(barrier, REMOTE + 3)
-
-    gate_up = {}
-    for d in (1, 3, 2):
-        for a, (h, v) in enumerate(((wg_hbm, wg), (wu_hbm, wu))):
-            gate_up[a, d] = remote(h.at[side[d]], v.at[d], wsend.at[a, d], wrecv.at[a, d], (e, side[d]))
-            gate_up[a, d].start()
-    source_copies = [remote(src, srcs.at[t], ssend.at[d], srecv.at[d], (e, side[d])) for d in (1, 2, 3)]
-    for cp in source_copies:
-        cp.start()
-    srcs[t] = src[...]
 
     slot_row = iota((GROUPS, 512), 0)
     wanted = jnp.full((GROUPS, 512), 4 * e + t, jnp.int32)
@@ -137,6 +127,34 @@
     rank = jnp.where(chosen > 0.5, rank, -1.0).astype(BF)
     weight = weight.astype(BF)
 
+    pl.semaphore_wait(barrier, REMOTE + 3)
+
+    source_copies = [remote(src, srcs.at[t], ssend.at[d], srecv.at[d], (e, side[d])) for d in (1, 2, 3)]
+    for cp in source_copies:
+        cp.start()
+    gate_up = {}
+    for n in (1, 2, 3):
+        d = STEP[n]
+        for a, (h, v) in enumerate(((wg_hbm, wg), (wu_hbm, wu))):
+            gate_up[a, n] = remote(h.at[side[d]], v.at[n], wsend.at[a, n], wrecv.at[a, n], (e, side[d]))
+            gate_up[a, n].start()
+    down = {}
+    for k in range(CHUNKS):
+        cols = pl.ds(k * CW, CW)
+        for n in (1, 2, 3):
+            d = STEP[n]
+            down[k, n] = remote(
+                wd_hbm.at[side[d], :, cols], wd.at[n, :, cols], wsend.at[2 + k, n], wrecv.at[2 + k, n], (e, side[d])
+            )
+            down[k, n].start()
+    for d in (1, 2, 3):
+
+        @pl.when(t + d < 4)
+        def _(d=d):
+            remote(codec_hbm, codec.at[t], csend.at[d], crecv.at[d], (e, side[d])).start()
+
+    srcs[t] = src[...]
+
     local[0].wait()
 
     def norm_tile(i, carry):
@@ -147,21 +165,21 @@
     lax.fori_loop(0, 8, norm_tile, 0)
 
     def dispatch_tile(i, carry):
-        rows = pl.ds(pl.multiple_of(i * 128, 128), 128)
-        spread = ones_where(((iota((128, GROUPS), 0) + i * 128) >> 5) == iota((128, GROUPS), 1))
-        place = (iota((128, 512), 0) & 31).astype(F32)
+        rows = pl.ds(pl.multiple_of(i * 256, 256), 256)
+        spread = ones_where(((iota((256, GROUPS), 0) + i * 256) >> 5) == iota((256, GROUPS), 1))
+        place = (iota((256, 512), 0) & 31).astype(F32)
         hit = mm(spread, rank) == place
         pw[rows, :] = jnp.where(hit, mm(spread, weight), 0.0).astype(BF)
         sb[rows, :] = mm(ones_where(hit), tok[...]).astype(BF)
         return carry
 
-    lax.fori_loop(0, 8, dispatch_tile, 0)
-    dispatch = []
-    for i in range(REMOTE):
-        cp = remote(
-            sb.at[pl.ds(i * SLOT, SLOT)], xb.at[pl.ds(i * SLOT, SLOT)], dsend.at[0], drecv.at[0], (to[i], t)
-        )
-        cp.start()
+    for g in range(4):
+        dispatch_tile(g, 0)
+        for i in range(8 * g, min(8 * g + 8, REMOTE)):
+            cp = remote(
+                sb.at[pl.ds(i * SLOT, SLOT)], xb.at[pl.ds(i * SLOT, SLOT)], dsend.at[0], drecv.at[g], (to[i], t)
+            )
+            cp.start()
 
     spread = ones_where((iota((64, GROUPS), 0) >> 1) == iota((64, GROUPS), 1))
     place = (iota((64, 512), 0) & 1).astype(F32) + 32.0
@@ -175,7 +193,7 @@
         packed = packed + mm(ones_where(same & (((row >> 1) & 7) == q)), extra[:, q * 256 : (q + 1) * 256])
     rem_s[...] = packed.astype(BF)
     for i in range(REMOTE):
-        cp = remote(rem_s.at[pl.ds(i * 16, 16)], rem_r.at[pl.ds(i * 16, 16)], dsend.at[1], drecv.at[1], (to[i], t))
+        cp = remote(rem_s.at[pl.ds(i * 16, 16)], rem_r.at[pl.ds(i * 16, 16)], dsend.at[1], drecv.at[4], (to[i], t))
         cp.start()
     xb[REMOTE * SLOT : 1024, :] = sb[REMOTE * SLOT : 1024, :]
     rem_r[REMOTE * 16 : 512, :] = rem_s[REMOTE * 16 : 512, :]
@@ -212,16 +230,28 @@
 
     lax.fori_loop(0, 4, pick_tile, 0)
 
-    remote(xb.at[pl.ds(0, REMOTE * SLOT)], xb.at[pl.ds(0, REMOTE * SLOT)], dsend.at[0], drecv.at[0], (to[0], t)).wait()
-    remote(rem_r.at[pl.ds(0, REMOTE * 16)], rem_r.at[pl.ds(0, REMOTE * 16)], dsend.at[1], drecv.at[1], (to[0], t)).wait()
-    down = {}
-    for k in range(CHUNKS):
-        cols = pl.ds(k * CW, CW)
-        for d in (1, 3, 2):
-            down[k, d] = remote(
-                wd_hbm.at[side[d], :, cols], wd.at[d, :, cols], wsend.at[2 + k, d], wrecv.at[2 + k, d], (e, side[d])
-            )
-            down[k, d].start()
+    local[1].wait()
+    local[2].wait()
+
+    def hidden(n, rows):
+        v = xb[rows, :]
+        g = mm_nt(v, wg[n])
+        u = mm_nt(v, wu[n])
+        hb[n, rows, :] = (g / (1.0 + jnp.exp(-g)) * u).astype(BF)
+
+    for n in (1, 2):
+        gate_up[0, n].wait()
+        gate_up[1, n].wait()
+    for g in range(4):
+        rows = pl.ds(g * 256, min(256, REMOTE * SLOT - g * 256))
+        remote(xb.at[rows], xb.at[rows], dsend.at[0], drecv.at[g], (to[0], t)).wait_recv()
+
+        def near(n, carry, g=g):
+            hidden(n, pl.ds(g * 256, 256))
+            return carry
+
+        lax.fori_loop(0, 3, near, 0)
+    remote(rem_r.at[pl.ds(0, REMOTE * 16)], rem_r.at[pl.ds(0, REMOTE * 16)], dsend.at[1], drecv.at[4], (to[0], t)).wait()
     row, col = iota((64, 512), 0), iota((64, 512), 1)
     same = ((col >> 4) == (row >> 1)) & ((row & 1) == (col & 1))
     for q in range(8):
@@ -229,22 +259,22 @@
             ones_where(same & (((col >> 1) & 7) == q)), rem_r[...]
         ).astype(BF)
 
-    for d in (0, 1, 3, 2):
-        if d == 0:
-            local[1].wait()
-            local[2].wait()
-        else:
-            gate_up[0, d].wait()
-            gate_up[1, d].wait()
-
-        def hidden_tile(i, carry, d=d):
-            rows = pl.ds(pl.multiple_of(i * 272, 16), 272)
-            g = mm_nt(xb[rows, :], wg[d])
-            u = mm_nt(xb[rows, :], wu[d])
-            hb[d, rows, :] = (g / (1.0 + jnp.exp(-g)) * u).astype(BF)
-            return carry
-
-        lax.fori_loop(0, 4, hidden_tile, 0)
+    def spare(n, carry):
+        hidden(n, pl.ds(1024, 64))
+        return carry
+
+    lax.fori_loop(0, 3, spare, 0)
+    gate_up[0, 3].wait()
+    gate_up[1, 3].wait()
+
+    def far(i, carry):
+        hidden(3, pl.ds(pl.multiple_of(i * 272, 16), 272))
+        return carry
+
+    lax.fori_loop(0, 4, far, 0)
+    remote(
+        sb.at[pl.ds(0, REMOTE * SLOT)], xb.at[pl.ds(0, REMOTE * SLOT)], dsend.at[0], drecv.at[0], (to[0], t)
+    ).wait_send()
 
     local[3].wait()
     row, col = iota((256, 64), 0), iota((256, 64), 1)
@@ -257,24 +287,18 @@
     ]
     for k in range(CHUNKS):
         cols = pl.ds(k * CW, CW)
-        for d in (1, 3, 2):
-            down[k, d].wait()
+        for n in (1, 2, 3):
+            down[k, n].wait()
 
         def out_tile(i, carry, cols=cols):
             rows = pl.ds(pl.multiple_of(i * 272, 16), 272)
             o = mm(hb[0, rows, :], wd[0, :, cols])
-            for d in (1, 3, 2):
-                o = o + mm(hb[d, rows, :], wd[d, :, cols])
+            for n in (1, 2, 3):
+                o = o + mm(hb[n, rows, :], wd[n, :, cols])
             sb[rows, cols] = o.astype(BF)
             return carry
 
         lax.fori_loop(0, 4, out_tile, 0)
-        for i in range(REMOTE):
-            cp = remote(
-                sb.at[pl.ds(i * SLOT, SLOT), cols], rb.at[pl.ds(i * SLOT, SLOT), cols],
-                rsend.at[0, k], rrecv.at[0, k], (back[i], t),
-            )
-            cp.start()
         last = sb[1024:1088, cols]
         packed = jnp.zeros((256, 128), F32)
         for q in range(4):
@@ -286,44 +310,87 @@
                 rsend.at[1, k], rrecv.at[1, k], (back[i], t),
             )
             cp.start()
+        for p, (begin, width, _) in enumerate(PIECES):
+            if begin // CW == k:
+                part = pl.ds(begin, width)
+                for i in range(REMOTE):
+                    cp = remote(
+                        sb.at[pl.ds(i * SLOT, SLOT), part], rb.at[pl.ds(i * SLOT, SLOT), part],
+                        rsend.at[0, p], rrecv.at[0, p], (back[i], t),
+                    )
+                    cp.start()
         rb[REMOTE * SLOT : 1024, cols] = sb[REMOTE * SLOT : 1024, cols]
         rrem[k, REMOTE * 8 : 256, :] = orem[k, REMOTE * 8 : 256, :]
-
-    local[8].wait()
-    for d in (1, 2, 3):
-
-        @pl.when(t + d < 4)
-        def _(d=d):
-            remote(codec.at[t], codec.at[t], csend.at[d], crecv.at[d], (e, side[d])).start()
 
     local[4].wait()
     sums = {}
     own = pl.ds(pl.multiple_of(t * 128, 128), 128)
     hacc[...] = jnp.zeros_like(hacc)
 
-    def finish_chunk(k):
-        cols = pl.ds(k * CW, CW)
-        total = ps[own, cols].astype(F32)
-        for d in (1, 2, 3):
-            sums[k, d].wait()
-            total = total + pr[d, :, cols].astype(F32)
+    pair = (t + 1 - 2 * (t % 2), 3 - t)
+    cross = lax.rem(t + 2, 4)
+
+    def block(who):
+        return pl.ds(pl.multiple_of(who * 128, 128), 128)
+
+    def halves(p):
+        return [(h, pl.ds(PIECES[p][0] + h * 256, 256), pair[h], pair[1 - h]) for h in (0, 1)]
+
+    def begin_sum(p):
+        begin, width, _ = PIECES[p]
+        if p < PAIRED:
+            for h, cols, one, _ in halves(p):
+                for n, who in ((1, cross), (0, one)):
+                    sums[p, h, n] = remote(
+                        ps.at[block(who), cols], pr.at[n, :, cols], psend.at[p, 2 * h + n], precv.at[p, 2 * h + n], (e, one)
+                    )
+                    sums[p, h, n].start()
+            return
+        cols = pl.ds(begin, width)
+        for d in (2, 1, 3):
+            sums[p, d] = remote(
+                ps.at[block(side[d]), cols], pr.at[d, :, cols], psend.at[p, d], precv.at[p, d], (e, side[d])
+            )
+            sums[p, d].start()
+
+    def middle(p):
+        for h, cols, one, two in halves(p):
+            sums[p, h, 1].wait()
+            pr[2, :, cols] = (ps[block(two), cols].astype(F32) + pr[1, :, cols].astype(F32)).astype(BF)
+            sums[p, h, 2] = remote(pr.at[2, :, cols], pr.at[3, :, cols], qsend.at[p, h], qrecv.at[p, h], (e, two))
+            sums[p, h, 2].start()
+
+    def finish(p):
+        begin, width, _ = PIECES[p]
+        cols = pl.ds(begin, width)
+        if p < PAIRED:
+            for h in (0, 1):
+                sums[p, h, 0].wait()
+                sums[p, h, 2].wait()
+            total = ps[own, cols].astype(F32) + pr[0, :, cols].astype(F32) + pr[3, :, cols].astype(F32)
+        else:
+            total = ps[own, cols].astype(F32)
+            for d in (1, 2, 3):
+                sums[p, d].wait()
+                total = total + pr[d, :, cols].astype(F32)
         done = total.astype(BF)
         thinker[:, cols] = done
         hacc[...] += mm(done, wh[cols, :])
 
-    for k in range(CHUNKS):
-        cols = pl.ds(k * CW, CW)
+    for p, (begin, width, k) in enumerate(PIECES):
+        cols = pl.ds(begin, width)
+        if k is not None:
+            remote(
+                orem.at[k, pl.ds(0, REMOTE * 8)], rrem.at[k, pl.ds(0, REMOTE * 8)],
+                rsend.at[1, k], rrecv.at[1, k], (to[0], t),
+            ).wait()
+            got = rrem[k].astype(BF)
+            for q in range(4):
+                rb[1024:1088, k * CW + q * 128 : k * CW + (q + 1) * 128] = mm(unpack[q], got).astype(BF)
         remote(
             sb.at[pl.ds(0, REMOTE * SLOT), cols], rb.at[pl.ds(0, REMOTE * SLOT), cols],
-            rsend.at[0, k], rrecv.at[0, k], (to[0], t),
+            rsend.at[0, p], rrecv.at[0, p], (to[0], t),
         ).wait()
-        remote(
-            orem.at[k, pl.ds(0, REMOTE * 8)], rrem.at[k, pl.ds(0, REMOTE * 8)],
-            rsend.at[1, k], rrecv.at[1, k], (to[0], t),
-        ).wait()
-        got = rrem[k].astype(BF)
-        for q in range(4):
-            rb[1024:1088, k * CW + q * 128 : k * CW + (q + 1) * 128] = mm(unpack[q], got).astype(BF)
 
         def sum_tile(i, carry, cols=cols):
             rows = pl.ds(pl.multiple_of(i * 128, 128), 128)
@@ -331,13 +398,15 @@
             return carry
 
         lax.fori_loop(0, 4, sum_tile, 0)
-        for d in (1, 2, 3):
-            rows = pl.ds(pl.multiple_of(side[d] * 128, 128), 128)
-            sums[k, d] = remote(ps.at[rows, cols], pr.at[d, :, cols], psend.at[k, d], precv.at[k, d], (e, side[d]))
-            sums[k, d].start()
-        if k > 0:
-            finish_chunk(k - 1)
-    finish_chunk(CHUNKS - 1)
+        begin_sum(p)
+        if 1 <= p <= PAIRED:
+            middle(p - 1)
+        if 2 <= p <= PAIRED:
+            finish(p - 2)
+        if p == PAIRED + 1:
+            finish(p - 2)
+            finish(p - 1)
+    finish(len(PIECES) - 1)
     ha[own, :] = hacc[...].astype(BF)
     handed = [remote(ha.at[own], ha.at[own], hsend.at[d], hrecv.at[d], (e, side[d])) for d in (1, 2, 3)]
     for cp in handed:
@@ -346,11 +415,11 @@
 
         @pl.when(t + d < 4)
         def _(d=d):
-            remote(codec.at[t], codec.at[t], csend.at[d], crecv.at[d], (e, side[d])).wait_send()
+            remote(codec_hbm, codec.at[t], csend.at[d], crecv.at[d], (e, side[d])).wait_send()
 
         @pl.when(t >= d)
         def _(d=d):
-            remote(codec.at[t - d], codec.at[t - d], csend.at[d], crecv.at[d], (e, side[d])).wait_recv()
+            remote(codec_hbm, codec.at[t - d], csend.at[d], crecv.at[d], (e, side[d])).wait_recv()
 
     for i in (5, 6, 7):
         local[i].wait()
@@ -372,18 +441,20 @@
     mine = pl.ds(pl.multiple_of(t * 256, 256), 256)
     queries = mm(tn[mine, :], wq[...])
     for h in range(8):
-        qb[:, h * 128 : (h + 1) * 128] = rms(queries[:, h * 128 : (h + 1) * 128], qkg[0:1, :]).astype(BF)
-
-    def head(h, carry):
-        lanes = pl.ds(pl.multiple_of(h * 128, 128), 128)
-        keys = kb[:, pl.ds(pl.multiple_of((h >> 1) * 128, 128), 128)]
-        s = mm_nt(qb[:, lanes], keys) * (128.0 ** -0.5) + bias[...]
-        w = jnp.exp(s - jnp.max(s, axis=-1, keepdims=True)).astype(BF)
-        o = mm(w, vb[:, pl.ds(pl.multiple_of((h >> 1) * 256, 256), 256)])
+        scaled = rms(queries[:, h * 128 : (h + 1) * 128], qkg[0:1, :] * (128.0**-0.5 * math.log2(math.e)))
+        qb[:, h * 128 : (h + 1) * 128] = scaled.astype(BF)
+
+    for h in range(8):
+        lanes = slice(h * 128, (h + 1) * 128)
+        g = h // 2
+        s = mm_nt(qb[:, lanes], kb[:, g * 128 : (g + 1) * 128]) + bias[...]
+        w = jnp.exp2(s - jnp.max(s, axis=-1, keepdims=True)).astype(BF)
+        o = mm(w, vb[:, g * 256 : (g + 1) * 256])
         at[:, lanes] = (o[:, :128] / o[:, 128:]).astype(BF)
-        return carry
-
-    lax.fori_loop(0, 8, head, 0)
+
+
+def project(at, wo, thinker_in, thinker, talker):
+    thinker[...] = thinker_in[...]
     talker[...] = mm(at[...], wo[...]).astype(BF)
 
 
@@ -401,7 +472,6 @@
         ((4, 192, 2048), BF),
         ((4, 192, 2048), BF),
         ((2048, 1024), BF),
-        ((1024, 1024), BF),
         ((1024, 1024), BF),
         ((1024, 1024), BF),
         ((1088, 512), BF),
@@ -426,17 +496,15 @@
         ((1024, 1024), BF),
         ((256, 1024), F32),
         ((256, 1024), BF),
-        ((256, 1024), BF),
-        ((8, 128), F32),
     ]
-    sems = [(9,), (6, 4), (6, 4), (2,), (2,), (2, 4), (2, 4), (4, 4), (4, 4), (4,), (4,), (4,), (4,), (4,), (4,)]
-    return pl.pallas_call(
+    sems = [(8,), (6, 4), (6, 4), (2,), (5,), (2, 5), (2, 5), (5, 4), (5, 4), (3, 2), (3, 2), (4,), (4,), (4,), (4,), (4,), (4,)]
+    thinker, attended = pl.pallas_call(
         kernel,
         out_shape=(
             jax.ShapeDtypeStruct((128, 2048), BF),
             jax.ShapeDtypeStruct((256, 1024), BF),
         ),
-        in_specs=[hb, vm, vm, vm, hb, hb, hb, hb, sm, vm, hb, vm, hb, hb, vm, hb],
+        in_specs=[hb, vm, vm, vm, hb, hb, hb, hb, sm, vm, hb, vm, hb, hb, vm],
         out_specs=(vm, vm),
         scratch_shapes=[pltpu.VMEM(s, d) for s, d in scratch] + [dma(s) for s in sems],
         compiler_params=pltpu.CompilerParams(
@@ -460,8 +528,19 @@
         w_query,
         w_kv,
         qk_gains,
-        w_out,
     )
+    return pl.pallas_call(
+        project,
+        out_shape=(
+            jax.ShapeDtypeStruct((128, 2048), BF),
+            jax.ShapeDtypeStruct((256, 1024), BF),
+        ),
+        in_specs=[vm, vm, vm],
+        out_specs=(vm, vm),
+        cost_estimate=pl.CostEstimate(flops=536_870_912, bytes_accessed=5_000_000, transcendentals=0),
+        compiler_params=pltpu.CompilerParams(vmem_limit_bytes=61 << 20),
+        name="project",
+    )(attended, w_out, thinker)
 
 
 def solution(mesh):

time: 197 us -> 178 us (0.904)
  Pallas kernels: 192 us -> 177 us
  local copies, waits for them, and re-layouts: 3.75 us -> 0 us
    pallas_call x1, Pallas kernels: 192 us -> 173 us  [per_device(): pl.pallas_call(kernel, out_shape=(jax.ShapeDtypeStruct((128, 2048), BF),...]
    unnamed x2 -> x0, local copies, waits for them, and re-layouts: 3.75 us -> none
    pallas_call x0 -> x1, Pallas kernels: none -> 3.46 us  [per_device(): pl.pallas_call(project, out_shape=(jax.ShapeDtypeStruct((128, 2048), BF),...]
where the time goes in v2:
time: 178 us
  Pallas kernels  177 us (99%)
    pallas_call x1, Pallas kernels, per_device(): pl.pallas_call(kernel, out_shape=(jax.ShapeDtypeStruct((128, 2048), BF),...  173 us

profile of v2, /device:TPU:0, one launch (start us, length us, event | category | flops | bytes accessed | tf_op | source)
XLA Modules:
  0.0 177.6 jit_solution(16135394417752607711)
XLA Ops:
  0.6 173.5 %expert_talker.1 = (bf16[128,2048]{1,0:T(8,128)(2,1)}, bf16[256,1024]{1,0:T(8,128)(2,1)}) custom-call(bf16[512,2048]{1,0:T(8,128)(2,1)} %tok_hbm.1, f32[1,2048]{1,0:T(1,128)} %bitcast.11, s32[8,512]{1,0:T(8,128)} %bitcast.9, f32[8,512]{1,0:T(8,128)} %bitcast.10, bf16[4,192,2048]{2,1,0:T(8,128)(2,1)} %bitcast.7, bf16[4,192,2048]{2,1,0:T(8,128)(2,1)} %bitcast.8, ...), custom_call_target="tpu_custom_call" | custom-call | flops 20000000000 | bytes 40000000 | tf_op jit(solution)/shard_map/expert_talker/pallas_call | solution.py:501
  174.1 3.5 %project.1 = (bf16[128,2048]{1,0:T(8,128)(2,1)}, bf16[256,1024]{1,0:T(8,128)(2,1)}) custom-call(bf16[256,1024]{1,0:T(8,128)(2,1)} %get-tuple-element.4.at, bf16[1024,1024]{1,0:T(8,128)(2,1)} %wo.1, bf16[128,2048]{1,0:T(8,128)(2,1)} %get-tuple-element.5.thinker_in), custom_call_target="tpu_custom_call" | custom-call | flops 536870912 | bytes 5000000 | tf_op jit(solution)/shard_map/project/pallas_call | solution.py:532

commit v3 on v2

--- a/solution.py
+++ b/solution.py
@@ -15,29 +15,20 @@
 SLOT = 32
 CHUNKS = 4
 CW = 512
-PIECES = ((0, 512, 0), (512, 512, 1), (1024, 512, 2), (1536, 256, 3), (1792, 256, None))
+PIECES = ((0, 512, 0), (512, 512, None), (1024, 512, 1), (1536, 256, None), (1792, 256, None))
 PAIRED = 3
 STEP = (0, 1, 3, 2)
 
 
 def peer_shifts():
-    def opposite(s):
-        return ((4 - s[0]) % 4, (4 - s[1]) % 4, s[2])
-
-    every = [
-        (dx, dz, dc)
-        for dx in range(4)
-        for dz in range(4)
-        for dc in range(2)
-        if (dx, dz, dc) != (0, 0, 0)
-    ]
-    order, seen = [], set()
-    for s in sorted(every, key=lambda s: (sum(min(v, 4 - v) for v in s[:2]), s)):
-        for one in (s, opposite(s)):
-            if one not in seen:
-                seen.add(one)
-                order.append(one)
-    return order[::-1]
+    order = []
+    for a, b in ((1, 2), (1, 1), (2, 2), (2, 0), (1, 0), (0, 0)):
+        for _ in range(4):
+            for c in (0, 1):
+                if (a, b, c) != (0, 0, 0) and (a, b, c) not in order:
+                    order.append((a, b, c))
+            a, b = (4 - b) % 4, a
+    return order
 
 
 SHIFTS = peer_shifts()
@@ -109,23 +100,6 @@
         return pltpu.make_async_remote_copy(
             src_ref=a, dst_ref=b, send_sem=s, recv_sem=r, device_id=device, device_id_type=MESH
         )
-
-    slot_row = iota((GROUPS, 512), 0)
-    wanted = jnp.full((GROUPS, 512), 4 * e + t, jnp.int32)
-    for i in range(REMOTE):
-        wanted = jnp.where(slot_row == i, 4 * to[i] + t, wanted)
-    total = jnp.sum(rw[...], axis=0, keepdims=True)
-    share = rw[...] / total
-    chosen = jnp.zeros((GROUPS, 512), F32)
-    weight = jnp.zeros((GROUPS, 512), F32)
-    for k in range(8):
-        hit = ids[k : k + 1, :] == wanted
-        chosen = chosen + jnp.where(hit, 1.0, 0.0)
-        weight = weight + jnp.where(hit, share[k : k + 1, :], 0.0)
-    upper = ones_where(iota((512, 512), 0) < iota((512, 512), 1))
-    rank = mm(chosen.astype(BF), upper)
-    rank = jnp.where(chosen > 0.5, rank, -1.0).astype(BF)
-    weight = weight.astype(BF)
 
     pl.semaphore_wait(barrier, REMOTE + 3)
 
@@ -155,6 +129,23 @@
 
     srcs[t] = src[...]
 
+    slot_row = iota((GROUPS, 512), 0)
+    wanted = jnp.full((GROUPS, 512), 4 * e + t, jnp.int32)
+    for i in range(REMOTE):
+        wanted = jnp.where(slot_row == i, 4 * to[i] + t, wanted)
+    total = jnp.sum(rw[...], axis=0, keepdims=True)
+    share = rw[...] / total
+    chosen = jnp.zeros((GROUPS, 512), F32)
+    weight = jnp.zeros((GROUPS, 512), F32)
+    for k in range(8):
+        hit = ids[k : k + 1, :] == wanted
+        chosen = chosen + jnp.where(hit, 1.0, 0.0)
+        weight = weight + jnp.where(hit, share[k : k + 1, :], 0.0)
+    upper = ones_where(iota((512, 512), 0) < iota((512, 512), 1))
+    rank = mm(chosen.astype(BF), upper)
+    rank = jnp.where(chosen > 0.5, rank, -1.0).astype(BF)
+    weight = weight.astype(BF)
+
     local[0].wait()
 
     def norm_tile(i, carry):
@@ -175,11 +166,11 @@
 
     for g in range(4):
         dispatch_tile(g, 0)
-        for i in range(8 * g, min(8 * g + 8, REMOTE)):
-            cp = remote(
-                sb.at[pl.ds(i * SLOT, SLOT)], xb.at[pl.ds(i * SLOT, SLOT)], dsend.at[0], drecv.at[g], (to[i], t)
-            )
-            cp.start()
+        for i, part in [
+            (i, pl.ds(k * CW, CW)) for k in range(CHUNKS) for i in range(8 * g, min(8 * g + 8, REMOTE))
+        ]:
+            slot = pl.ds(i * SLOT, SLOT)
+            remote(sb.at[slot, part], xb.at[slot, part], dsend.at[0], drecv.at[g], (to[i], t)).start()
 
     spread = ones_where((iota((64, GROUPS), 0) >> 1) == iota((64, GROUPS), 1))
     place = (iota((64, 512), 0) & 1).astype(F32) + 32.0
@@ -277,14 +268,12 @@
     ).wait_send()
 
     local[3].wait()
-    row, col = iota((256, 64), 0), iota((256, 64), 1)
-    pack = [
-        ones_where(((row >> 3) == (col >> 1)) & ((row & 1) == (col & 1)) & (((row >> 1) & 3) == q)) for q in range(4)
-    ]
-    row, col = iota((64, 256), 0), iota((64, 256), 1)
-    unpack = [
-        ones_where(((col >> 3) == (row >> 1)) & ((row & 1) == (col & 1)) & (((col >> 1) & 3) == q)) for q in range(4)
-    ]
+    row, col = iota((512, 64), 0), iota((512, 64), 1)
+    pack_same = ((row >> 4) == (col >> 1)) & ((row & 1) == (col & 1))
+    pack_q = (row >> 1) & 7
+    row, col = iota((64, 512), 0), iota((64, 512), 1)
+    unpack_same = ((col >> 4) == (row >> 1)) & ((row & 1) == (col & 1))
+    unpack_q = (col >> 1) & 7
     for k in range(CHUNKS):
         cols = pl.ds(k * CW, CW)
         for n in (1, 2, 3):
@@ -299,17 +288,22 @@
             return carry
 
         lax.fori_loop(0, 4, out_tile, 0)
-        last = sb[1024:1088, cols]
-        packed = jnp.zeros((256, 128), F32)
-        for q in range(4):
-            packed = packed + mm(pack[q], last[:, q * 128 : (q + 1) * 128])
-        orem[k] = packed
-        for i in range(REMOTE):
-            cp = remote(
-                orem.at[k, pl.ds(i * 8, 8)], rrem.at[k, pl.ds(i * 8, 8)],
-                rsend.at[1, k], rrecv.at[1, k], (back[i], t),
-            )
-            cp.start()
+        if k % 2 == 1:
+            m = k // 2
+            packed = jnp.zeros((512, 128), F32)
+            for q in range(8):
+                packed = packed + mm(
+                    ones_where(pack_same & (pack_q == q)),
+                    sb[1024:1088, m * 1024 + q * 128 : m * 1024 + (q + 1) * 128],
+                )
+            orem[m] = packed.astype(BF)
+            for i in range(REMOTE):
+                cp = remote(
+                    orem.at[m, pl.ds(i * 16, 16)], rrem.at[m, pl.ds(i * 16, 16)],
+                    rsend.at[1, m], rrecv.at[1, m], (back[i], t),
+                )
+                cp.start()
+            rrem[m, REMOTE * 16 : 512, :] = orem[m, REMOTE * 16 : 512, :]
         for p, (begin, width, _) in enumerate(PIECES):
             if begin // CW == k:
                 part = pl.ds(begin, width)
@@ -320,7 +314,6 @@
                     )
                     cp.start()
         rb[REMOTE * SLOT : 1024, cols] = sb[REMOTE * SLOT : 1024, cols]
-        rrem[k, REMOTE * 8 : 256, :] = orem[k, REMOTE * 8 : 256, :]
 
     local[4].wait()
     sums = {}
@@ -377,16 +370,17 @@
         thinker[:, cols] = done
         hacc[...] += mm(done, wh[cols, :])
 
-    for p, (begin, width, k) in enumerate(PIECES):
+    for p, (begin, width, m) in enumerate(PIECES):
         cols = pl.ds(begin, width)
-        if k is not None:
+        if m is not None:
             remote(
-                orem.at[k, pl.ds(0, REMOTE * 8)], rrem.at[k, pl.ds(0, REMOTE * 8)],
-                rsend.at[1, k], rrecv.at[1, k], (to[0], t),
+                orem.at[m, pl.ds(0, REMOTE * 16)], rrem.at[m, pl.ds(0, REMOTE * 16)],
+                rsend.at[1, m], rrecv.at[1, m], (to[0], t),
             ).wait()
-            got = rrem[k].astype(BF)
-            for q in range(4):
-                rb[1024:1088, k * CW + q * 128 : k * CW + (q + 1) * 128] = mm(unpack[q], got).astype(BF)
+            for q in range(8):
+                rb[1024:1088, m * 1024 + q * 128 : m * 1024 + (q + 1) * 128] = mm(
+                    ones_where(unpack_same & (unpack_q == q)), rrem[m]
+                ).astype(BF)
         remote(
             sb.at[pl.ds(0, REMOTE * SLOT), cols], rb.at[pl.ds(0, REMOTE * SLOT), cols],
             rsend.at[0, p], rrecv.at[0, p], (to[0], t),
@@ -408,7 +402,7 @@
             finish(p - 1)
     finish(len(PIECES) - 1)
     ha[own, :] = hacc[...].astype(BF)
-    handed = [remote(ha.at[own], ha.at[own], hsend.at[d], hrecv.at[d], (e, side[d])) for d in (1, 2, 3)]
+    handed = [remote(ha.at[own], ha.at[own], hsend.at[d], hrecv.at[d], (e, side[d])) for d in (2, 1, 3)]
     for cp in handed:
         cp.start()
     for d in (1, 2, 3):
@@ -453,9 +447,17 @@
         at[:, lanes] = (o[:, :128] / o[:, 128:]).astype(BF)
 
 
-def project(at, wo, thinker_in, thinker, talker):
-    thinker[...] = thinker_in[...]
+def project(at_hbm, wo_hbm, thinker_hbm, thinker, talker, at, wo, sem):
+    first = pltpu.make_async_copy(at_hbm, at, sem.at[0])
+    second = pltpu.make_async_copy(thinker_hbm, thinker, sem.at[1])
+    third = pltpu.make_async_copy(wo_hbm, wo, sem.at[2])
+    first.start()
+    third.start()
+    second.start()
+    first.wait()
+    third.wait()
     talker[...] = mm(at[...], wo[...]).astype(BF)
+    second.wait()
 
 
 def per_device(
@@ -482,8 +484,8 @@
         ((1088, 2048), BF),
         ((512, 256), BF),
         ((512, 256), BF),
-        ((4, 256, 128), F32),
-        ((4, 256, 128), F32),
+        ((2, 512, 128), BF),
+        ((2, 512, 128), BF),
         ((512, 2048), BF),
         ((4, 128, 2048), BF),
         ((128, 1024), F32),
@@ -535,8 +537,9 @@
             jax.ShapeDtypeStruct((128, 2048), BF),
             jax.ShapeDtypeStruct((256, 1024), BF),
         ),
-        in_specs=[vm, vm, vm],
+        in_specs=[hb, hb, hb],
         out_specs=(vm, vm),
+        scratch_shapes=[pltpu.VMEM((256, 1024), BF), pltpu.VMEM((1024, 1024), BF), dma((3,))],
         cost_estimate=pl.CostEstimate(flops=536_870_912, bytes_accessed=5_000_000, transcendentals=0),
         compiler_params=pltpu.CompilerParams(vmem_limit_bytes=61 << 20),
         name="project",

time: 178 us -> 179 us (level)
  no operation moved by 1% of the time
where the time goes in v3:
time: 179 us; the launch traced here: 178 us
  Pallas kernels  177 us (99%)
    pallas_call x1, Pallas kernels, per_device(): pl.pallas_call(kernel, out_shape=(jax.ShapeDtypeStruct((128, 2048), BF),...  173 us

profile of v3, /device:TPU:0, one launch (start us, length us, event | category | flops | bytes accessed | tf_op | source)
XLA Modules:
  0.0 177.5 jit_solution(12158102396113293500)
XLA Ops:
  0.6 173.3 %expert_talker.1 = (bf16[128,2048]{1,0:T(8,128)(2,1)}, bf16[256,1024]{1,0:T(8,128)(2,1)}) custom-call(bf16[512,2048]{1,0:T(8,128)(2,1)} %tok_hbm.1, f32[1,2048]{1,0:T(1,128)} %bitcast.11, s32[8,512]{1,0:T(8,128)} %bitcast.9, f32[8,512]{1,0:T(8,128)} %bitcast.10, bf16[4,192,2048]{2,1,0:T(8,128)(2,1)} %bitcast.7, bf16[4,192,2048]{2,1,0:T(8,128)(2,1)} %bitcast.8, ...), custom_call_target="tpu_custom_call" | custom-call | flops 20000000000 | bytes 40000000 | tf_op jit(solution)/shard_map/expert_talker/pallas_call | solution.py:503
  173.9 3.5 %project.1 = (bf16[128,2048]{1,0:T(8,128)(2,1)}, bf16[256,1024]{1,0:T(8,128)(2,1)}) custom-call(bf16[256,1024]{1,0:T(8,128)(2,1)} %get-tuple-element.4.at_hbm, bf16[1024,1024]{1,0:T(8,128)(2,1)} %wo_hbm.1, bf16[128,2048]{1,0:T(8,128)(2,1)} %get-tuple-element.5.thinker_hbm), custom_call_target="tpu_custom_call" | custom-call | flops 536870912 | bytes 5000000 | tf_op jit(solution)/shard_map/project/pallas_call | solution.py:534
